TPU v7x, 32 devices: a whole 2x2x4 slice. The times are simulated.
32 devices in a mesh: groups: 2 (over x), exp: 8 (over z, y), seq: 2 (over core).
Axes of the slice: x: 2, y: 2, z: 4, core: 2. Of those that a mesh axis runs over, the one named last changes fastest.
Arguments:
- queries: bfloat16 [4096, 3584], P(('groups', 'exp'), 'seq'), parts along dimension 0, may hold values from -6 to 6
- key_rows: bfloat16 [4096, 3584], P(('groups', 'exp'), 'seq'), parts along dimension 0, may hold values from -6 to 6
- value_rows: bfloat16 [4096, 3584], P(('groups', 'exp'), 'seq'), parts along dimension 0, may hold values from -6 to 6
- residual: bfloat16 [4096, 3584], P(('groups', 'exp', 'seq')), parts along dimension 0, may hold values from -9 to 9
- norm_gain: float32 [3584], replicated, may hold values from 0.1 to 1.9
- router_weight: bfloat16 [3584, 8], replicated, may hold values from -0.09375 to 0.09375
- expert_ids: int32 [4096, 4], P(('groups', 'exp', 'seq')), parts along dimension 0, may hold values from 0 to 7, as said below
- gate_proj: bfloat16 [8, 3584, 768], P('exp', None, 'seq'), may hold values from -0.09375 to 0.09375
- up_proj: bfloat16 [8, 3584, 768], P('exp', None, 'seq'), may hold values from -0.09375 to 0.09375
- down_proj: bfloat16 [8, 768, 3584], P('exp', 'seq'), may hold values from -0.4375 to 0.4375
Outputs:
- mixed: bfloat16 [4096, 3584], P(('groups', 'exp', 'seq')), parts along dimension 0
There are 2 independent parts, one for each index of `groups`. A program takes and returns all parts, laid end to end along the dimension named above; an argument that names none is the same for every part. Nothing has to cross between parts.
Inputs may be any that keep to these rules, and one draw needn't show every extreme that they name: `expert_ids`: each row names 4 different experts. Among the 512 entries of an aligned block of 128 tokens (the tokens of one device), no expert is named more than 96 times, and one expert is named exactly 96 times in every block.
All inputs are finite; a program needn't handle non-finite values.
Results may differ from a plain program's by a relative error of at most 0.014.
Values may be sent and summed in bfloat16 or wider, within the bound.
A program may use at most 128 MiB of HBM per device.

v0:
```python
import jax
import jax.numpy as jnp
from jax import lax
from jax.sharding import PartitionSpec as P

HDIM = 128
TOP = 4


epsilon = 1e-06


def head_attention(query_block, key_block, value_block):
    scores = jnp.einsum(
        "qhd,khd->hqk", query_block, key_block, preferred_element_type=jnp.float32
    ) * HDIM ** (-0.5)
    row_top = jnp.max(scores, axis=-1, keepdims=True)
    exp_scores = jnp.exp(scores - row_top)
    row_total = jnp.sum(exp_scores, axis=-1)
    mixed_heads = (
        jnp.einsum(
            "hqk,khd->qhd",
            exp_scores.astype(jnp.bfloat16),
            value_block,
            preferred_element_type=jnp.float32,
        )
        / jnp.transpose(row_total)[:, :, None]
    )
    return mixed_heads.astype(jnp.bfloat16)


def expert_partial(row_block, gate_cols, up_cols, down_rows):
    gate_out = jnp.dot(row_block, gate_cols, preferred_element_type=jnp.float32)
    up_out = jnp.dot(row_block, up_cols, preferred_element_type=jnp.float32)
    middle = (jax.nn.silu(gate_out) * up_out).astype(jnp.bfloat16)
    return jnp.dot(middle, down_rows, preferred_element_type=jnp.float32)


def on_device(
    queries,
    key_rows,
    value_rows,
    residual,
    norm_gain,
    router_weight,
    expert_ids,
    gate_proj,
    up_proj,
    down_proj,
):
    local_tokens = residual.shape[0]
    model_width = residual.shape[1]
    latent_rows = queries.shape[0]
    head_cols = queries.shape[1]
    heads_here = head_cols // HDIM
    local_heads = head_attention(
        queries.reshape(latent_rows, heads_here, HDIM),
        key_rows.reshape(latent_rows, heads_here, HDIM),
        value_rows.reshape(latent_rows, heads_here, HDIM),
    )
    attended = lax.all_to_all(
        local_heads.reshape(latent_rows, head_cols), "seq", split_axis=0, concat_axis=1, tiled=True
    )
    hidden = (residual.astype(jnp.float32) + attended.astype(jnp.float32)).astype(jnp.bfloat16)
    hidden_f = hidden.astype(jnp.float32)
    mean_sq = jnp.mean(hidden_f * hidden_f, axis=-1, keepdims=True)
    normed = (hidden_f * lax.rsqrt(mean_sq + epsilon) * norm_gain).astype(jnp.bfloat16)
    logits = jnp.dot(normed, router_weight, preferred_element_type=jnp.float32)
    experts = router_weight.shape[1]
    capacity = 3 * local_tokens * TOP // (2 * experts)
    catalog = jnp.arange(experts, dtype=jnp.int32)
    flat_ids = expert_ids.reshape(local_tokens * TOP)
    onehot = (flat_ids[:, None] == catalog[None, :]).astype(jnp.int32)
    picked = jnp.sum(
        onehot.reshape(local_tokens, TOP, experts).astype(jnp.float32) * logits[:, None, :], axis=2
    )
    sigmoids = jax.nn.sigmoid(picked)
    gate_values = sigmoids / jnp.sum(sigmoids, axis=1, keepdims=True)
    earlier = jnp.cumsum(onehot, axis=0) - onehot
    slot_index = jnp.sum(earlier * onehot, axis=1)
    place = flat_ids * capacity + slot_index
    source_rows = jnp.repeat(normed, TOP, axis=0)
    outgoing = (
        jnp.zeros((experts * capacity, model_width), jnp.bfloat16)
        .at[place]
        .set(source_rows)
        .reshape(experts, capacity, model_width)
    )
    both_halves = lax.all_gather(
        lax.all_to_all(outgoing, "exp", split_axis=0, concat_axis=0, tiled=True),
        "seq",
        axis=0,
        tiled=True,
    )
    partial_value = expert_partial(
        both_halves.reshape(-1, model_width), gate_proj[0], up_proj[0], down_proj[0]
    ).reshape(both_halves.shape)
    summed = lax.psum_scatter(
        partial_value.astype(jnp.bfloat16), "seq", scatter_dimension=0, tiled=True
    )
    answers = lax.all_to_all(summed, "exp", split_axis=0, concat_axis=0, tiled=True)
    returned_rows = answers.reshape(experts * capacity, model_width)
    gathered = returned_rows[place].reshape(local_tokens, TOP, model_width)
    moe_sum = hidden_f
    for which_slot in range(TOP):
        moe_sum = moe_sum + gate_values[:, which_slot : which_slot + 1] * gathered[
            :, which_slot
        ].astype(jnp.float32)
    return moe_sum.astype(jnp.bfloat16)


def solution(mesh):
    return jax.shard_map(
        on_device,
        mesh=mesh,
        in_specs=(
            P(("groups", "exp"), "seq"),
            P(("groups", "exp"), "seq"),
            P(("groups", "exp"), "seq"),
            P(("groups", "exp", "seq"), None),
            P(),
            P(),
            P(("groups", "exp", "seq"), None),
            P("exp", None, "seq"),
            P("exp", None, "seq"),
            P("exp", "seq", None),
        ),
        out_specs=P(("groups", "exp", "seq"), None),
        check_vma=False,
    )
```

profile of v0, /device:TPU:0, one launch (start us, length us, event | category | flops | bytes accessed | tf_op | source)
XLA Modules:
  0.0 450.0 jit_solution(15760562964701207874)
XLA Ops:
  6.5 0.0 copy-start
  6.5 2.4 copy.81
  8.9 2.2 copy.82
  11.2 2.2 copy.85
  13.4 2.1 multiply_reduce_fusion
  15.5 0.0 copy-start.4
  15.5 0.6 fusion
  16.2 0.5 copy-done.4
  16.7 2.2 fusion.19
  18.9 2.2 copy.88
  21.1 2.9 all_to_all.16
  24.0 2.2 copy.89
  26.2 4.4 all-to-all-start
  30.6 0.0 copy-start.7
  30.6 0.2 all-gather.2.cloned.1.call-start
  30.9 0.0 copy-done.6
  30.9 0.1 copy.91
  31.0 0.1 eq.39
  31.1 0.1 eq.35
  31.2 0.1 copy.90
  31.3 0.1 mul.112
  31.4 1.1 reduce-window.6
  32.6 0.2 slice_reduce_fusion
  32.8 2.2 copy.80
  35.1 0.0 all-to-all-done
  35.1 2.0 fusion.9
  37.1 0.0 copy-done.7
  37.1 0.0 copy-done.2
  37.1 2.7 fusion.11
  39.8 0.0 copy-done.8
  39.8 2.2 copy.93
  42.0 3.9 broadcast_in_dim.5
  46.0 6.7 %reshape.135 = bf16[512,3584]{1,0:T(8,128)(2,1)} reshape(bf16[128,4,3584]{2,1,0:T(4,128)(2,1)} %broadcast_in_dim.5) | data formatting | bytes 7340032 | tf_op jit(solution)/shard_map/reshape | solution.py:82
  52.7 0.0 slice-done
  52.7 0.1 fusion.25
  52.8 10.2 %scatter_custom_fusion = bf16[768,3584]{1,0:T(8,128)(2,1)} fusion(s32[512]{0:T(512)S(1)} %bitcast.80, bf16[512,3584]{1,0:T(8,128)(2,1)} %reshape.135, bf16[]{:T(256)} %constant.8.clone.1), kind=kCustom, calls=%fused_computation.13 | custom fusion | bytes 5505536 | tf_op jit(solution)/shard_map/scatter | solution.py:86
  63.0 129.0 %all_to_all.23 = bf16[8,96,3584]{2,1,0:T(8,128)(2,1)} all-to-all(bf16[8,96,3584]{2,1,0:T(8,128)(2,1)} %bitcast.75), channel_id=1, replica_groups=mesh['groups'=2,'exp'=8,'seq'=2] {'exp'}, dimensions={0} | all-to-all | bytes 11010048 | tf_op jit(solution)/shard_map/all_to_all | solution.py:90
  192.0 0.0 all-gather.2.cloned.1.call-update
  192.1 0.3 reduce-scatter.2.cloned.1.call-start
  192.3 22.3 %all-gather.2.cloned.1.call-done = bf16[16,96,3584]{2,1,0:T(8,128)(2,1)} async-done(((bf16[8,96,3584]{2,1,0:T(8,128)(2,1)}), bf16[16,96,3584]{2,1,0:T(8,128)(2,1)}) %all-gather.2.cloned.1.call-update) | async-done | bytes 11010064 | tf_op jit(solution)/shard_map/all_gather | solution.py:89
  214.6 9.7 %fusion.5 = f32[1536,384]{1,0:T(8,128)S(1)} fusion(bf16[1536,3584]{1,0:T(8,128)(2,1)} %bitcast.83, bf16[1,3584,384]{2,1,0:T(8,128)(2,1)} %param.17), kind=kOutput, calls=%fused_computation.11 | convolution fusion | flops 4227858432 | bytes 16121856 | tf_op jit(solution)/shard_map/dot_general | solution.py:33
  224.3 0.0 copy-done.9
  224.3 0.0 copy-done.10
  224.3 6.3 %fusion.2 = bf16[1536,384]{1,0:T(8,128)(2,1)S(1)} fusion(bf16[1536,3584]{1,0:T(8,128)(2,1)S(1)} %bitcast.84, bf16[1,3584,384]{2,1,0:T(8,128)(2,1)S(1)} %copy-done.10, f32[1536,384]{1,0:T(8,128)S(1)} %fusion.5), kind=kOutput, calls=%fused_computation.8 | convolution fusion | flops 4231397376 | bytes 17301504 | tf_op jit(solution)/shard_map/dot_general | solution.py:34
  230.7 0.0 copy-done
  230.7 8.5 %convolution_convert_fusion = bf16[16,96,3584]{2,1,0:T(8,128)(2,1)} fusion(bf16[16,96,384]{2,1,0:T(8,128)(2,1)S(1)} %bitcast.85, bf16[1,384,3584]{2,1,0:T(8,128)(2,1)S(1)} %copy-done), kind=kOutput, calls=%fused_computation.2 | convolution fusion | flops 4233363456 | bytes 14942208 | tf_op jit(solution)/shard_map/dot_general | solution.py:36
  239.2 0.0 reduce-scatter.2.cloned.1.call-update
  239.2 0.0 copy-start.3
  239.3 0.0 copy-start.5
  239.3 20.9 %reduce-scatter.2.cloned.1.call-done = bf16[8,96,3584]{2,1,0:T(8,128)(2,1)} async-done(((bf16[16,96,3584]{2,1,0:T(8,128)(2,1)}), bf16[8,96,3584]{2,1,0:T(8,128)(2,1)}) %reduce-scatter.2.cloned.1.call-update) | async-done | bytes 5505040 | tf_op jit(solution)/shard_map/reduce_scatter | solution.py:98
  260.2 5.8 %all-to-all-start.2 = ((bf16[8,96,3584]{2,1,0:T(8,128)(2,1)}), bf16[8,96,3584]{2,1,0:T(8,128)(2,1)}, u32[]{:S(2)}, u32[]{:S(2)}) async-start(bf16[8,96,3584]{2,1,0:T(8,128)(2,1)} %reduce-scatter.2.cloned.1.call-done), calls=%async_computation.3 | async-start | bytes 11010048 | tf_op jit(solution)/shard_map/all_to_all | solution.py:101
  266.0 0.0 copy-done.3
  266.0 0.0 copy-done.5
  266.0 0.2 fusion.29
  266.4 121.4 %all-to-all-done.2 = bf16[8,96,3584]{2,1,0:T(8,128)(2,1)} async-done(((bf16[8,96,3584]{2,1,0:T(8,128)(2,1)}), bf16[8,96,3584]{2,1,0:T(8,128)(2,1)}, u32[]{:S(2)}, u32[]{:S(2)}) %all-to-all-start.2) | async-done | bytes 5505056 | tf_op jit(solution)/shard_map/all_to_all | solution.py:101
  387.8 11.2 %gather_fusion = bf16[512,3584]{1,0:T(8,128)(2,1)} fusion(bf16[768,3584]{1,0:T(8,128)(2,1)} %bitcast.19, s32[1024]{0:T(1024)S(1)} %pad_clamp_fusion), kind=kCustom, calls=%fused_computation | custom fusion | bytes 7342080 | tf_op jit(solution)/shard_map/gather | solution.py:103
  399.1 7.0 %reshape.117 = bf16[128,4,3584]{2,1,0:T(4,128)(2,1)} reshape(bf16[512,3584]{1,0:T(8,128)(2,1)} %gather_fusion) | data formatting | bytes 7340032 | tf_op jit(solution)/shard_map/reshape | solution.py:103
  406.1 13.0 %fusion.28 = (bf16[128,1,3584]{2,1,0:T(2,128)(2,1)}, bf16[128,1,3584]{2,1,0:T(2,128)(2,1)}, bf16[128,1,3584]{2,1,0:T(2,128)(2,1)}, bf16[128,1,3584]{2,1,0:T(2,128)(2,1)S(1)}) fusion(bf16[128,4,3584]{2,1,0:T(4,128)(2,1)} %reshape.117), kind=kLoop, calls=%fused_computation.57 | loop fusion | bytes 7340032 | tf_op jit(solution)/shard_map/slice | solution.py:106
  419.1 4.8 %copy.103 = bf16[128,1,3584]{0,2,1:T(8,128)(2,1)} copy(bf16[128,1,3584]{2,1,0:T(2,128)(2,1)} %get-tuple-element.5) | data formatting | bytes 1835008
  423.8 4.8 %copy.105 = bf16[128,1,3584]{0,2,1:T(8,128)(2,1)} copy(bf16[128,1,3584]{2,1,0:T(2,128)(2,1)} %get-tuple-element.6) | data formatting | bytes 1835008
  428.6 4.8 %copy.104 = bf16[128,1,3584]{0,2,1:T(8,128)(2,1)} copy(bf16[128,1,3584]{2,1,0:T(2,128)(2,1)} %get-tuple-element.7) | data formatting | bytes 1835008
  433.4 2.9 copy.106
  436.4 4.6 %fusion.15 = bf16[128,3584]{0,1:T(8,128)(2,1)} fusion(bf16[128,1,3584]{0,2,1:T(8,128)(2,1)} %copy.106, bf16[128,1,3584]{0,2,1:T(8,128)(2,1)} %copy.105, bf16[128,1,3584]{0,2,1:T(8,128)(2,1)} %copy.104, bf16[128,1,3584]{0,2,1:T(8,128)(2,1)} %copy.103, f32[128]{0:T(128)S(1)} %get-tuple-element.10, f32[128]{0:T(128)S(1)} %get-tuple-element.11, ...), kind=kLoop, calls=%fused_computation.24 | loop fusion | flops 8257536 | bytes 6424576 | tf_op jit(solution)/shard_map/convert_element_type | solution.py:109
  441.0 2.2 copy.98
  (18 shorter events, 0.1 us)
Async XLA Ops:
  6.5 224.2 %copy-start = (bf16[1,384,3584]{2,1,0:T(8,128)(2,1)S(1)}, bf16[1,384,3584]{2,1,0:T(8,128)(2,1)}, u32[]{:S(2)}) copy-start(bf16[1,384,3584]{2,1,0:T(8,128)(2,1)} %param.19) | copy-start | bytes 8257540
  15.5 1.2 copy-start.4
  21.1 9.8 %copy-start.6 = (s32[128,4]{0,1:T(4,128)S(1)}, s32[128,4]{0,1:T(4,128)}, u32[]{:S(2)}) copy-start(s32[128,4]{0,1:T(4,128)} %param.16) | copy-start | bytes 6148
  26.2 8.8 %all-to-all-start = ((bf16[2,128,1792]{1,2,0:T(8,128)(2,1)}), bf16[2,128,1792]{1,2,0:T(8,128)(2,1)}, u32[]{:S(2)}, u32[]{:S(2)}) async-start(bf16[2,128,1792]{1,2,0:T(8,128)(2,1)} %copy.89), calls=%async_computation | async-start | bytes 1835008 | tf_op jit(solution)/shard_map/all_to_all | solution.py:61
  30.6 6.5 %copy-start.7 = (f32[3584]{0:T(1024)S(1)}, f32[3584]{0:T(1024)}, u32[]{:S(2)}) copy-start(f32[3584]{0:T(1024)} %param.14) | copy-start | bytes 43012
  30.6 184.0 %all-gather.2.cloned.1.call-start = ((), (), s32[]{:S(2)}) async-start(), calls=%async_computation.4 | async-start | bytes 16515072 | tf_op jit(solution)/shard_map/all_gather | solution.py:89
  32.8 7.0 %copy-start.8 = (s32[8,5]{0,1:T(8,128)}, s32[8,5]{0,1:T(8,128)S(1)}, u32[]{:S(2)}) copy-start(s32[8,5]{0,1:T(8,128)S(1)} %reduce-window.9) | copy-start | bytes 484
  35.1 2.0 copy-start.2
  46.0 6.7 %slice-start = ((s32[8,5]{0,1:T(8,128)}), s32[8,4]{0,1:T(4,128)S(1)}, s32[]{:S(2)}) async-start(s32[8,5]{0,1:T(8,128)} %copy-done.8), calls=%async_computation.6 | async-start | bytes 4096 | tf_op jit(solution)/shard_map/slice.1
  192.1 68.1 %reduce-scatter.2.cloned.1.call-start = ((), (), s32[]{:S(2)}) async-start(), calls=%async_computation.5 | async-start | bytes 16515072 | tf_op jit(solution)/shard_map/reduce_scatter | solution.py:98
  214.6 9.7 %copy-start.9 = (bf16[16,96,3584]{2,1,0:T(8,128)(2,1)S(1)}, bf16[16,96,3584]{2,1,0:T(8,128)(2,1)}, u32[]{:S(2)}) copy-start(bf16[16,96,3584]{2,1,0:T(8,128)(2,1)} %all-gather.2.cloned.1.call-done) | copy-start | bytes 33030148
  214.6 9.7 %copy-start.10 = (bf16[1,3584,384]{2,1,0:T(8,128)(2,1)S(1)}, bf16[1,3584,384]{2,1,0:T(8,128)(2,1)}, u32[]{:S(2)}) copy-start(bf16[1,3584,384]{2,1,0:T(8,128)(2,1)} %param.18) | copy-start | bytes 8257540
  239.2 26.8 %copy-start.3 = (bf16[128,3584]{0,1:T(8,128)(2,1)S(1)}, bf16[128,3584]{0,1:T(8,128)(2,1)}, u32[]{:S(2)}) copy-start(bf16[128,3584]{0,1:T(8,128)(2,1)} %fusion.11) | copy-start | bytes 2752516
  239.3 26.8 %copy-start.5 = (bf16[3584,8]{0,1:T(8,128)(2,1)S(1)}, bf16[3584,8]{0,1:T(8,128)(2,1)}, u32[]{:S(2)}) copy-start(bf16[3584,8]{0,1:T(8,128)(2,1)} %param.15) | copy-start | bytes 172036
  260.2 127.6 %all-to-all-start.2 = ((bf16[8,96,3584]{2,1,0:T(8,128)(2,1)}), bf16[8,96,3584]{2,1,0:T(8,128)(2,1)}, u32[]{:S(2)}, u32[]{:S(2)}) async-start(bf16[8,96,3584]{2,1,0:T(8,128)(2,1)} %reduce-scatter.2.cloned.1.call-done), calls=%async_computation.3 | async-start | bytes 11010048 | tf_op jit(solution)/shard_map/all_to_all | solution.py:101
  436.3 6.8 %copy-start.1 = (bf16[1,384,3584]{2,1,0:T(8,128)(2,1)S(1)}, bf16[1,384,3584]{2,1,0:T(8,128)(2,1)}, u32[]{:S(2)}) copy-start(bf16[1,384,3584]{2,1,0:T(8,128)(2,1)} %param.19) | copy-start | bytes 8257540
Sparse Core Ops, SparseCore 0:
  192.2 22.4 all-gather.1
  239.4 20.7 reduce-scatter.1
where the time goes:
time: 451 us; the launch traced here: 450 us
  waiting for transfers between devices  165 us (37%)
  blocking collectives  129 us (29%)
  local copies, waits for them, and re-layouts  91.6 us (20%)
  matrix products  29.1 us (6%)
  between operations  13.6 us (3%)
  other arithmetic  11.3 us (3%)
  starting transfers between devices  10.7 us (2%)
    all_to_all x1, blocking collectives, on_device(): lax.all_to_all(outgoing, 'exp', split_axis=0, concat_axis=0, tiled=True)  129 us
    all_to_all x1, waiting for transfers between devices, on_device(): lax.all_to_all(summed, 'exp', split_axis=0, concat_axis=0, tiled=True)  121 us
    unnamed x31, local copies, waits for them, and re-layouts  27 us
    all_gather x1, waiting for transfers between devices, on_device(): lax.all_gather(lax.all_to_all(outgoing, 'exp', split_axis=0, concat_axis=...  22.3 us
    reduce_scatter x1, waiting for transfers between devices, on_device(): lax.psum_scatter(partial_value.astype(jnp.bfloat16), 'seq', scatter_dimen...  20.9 us
    slice x1, local copies, waits for them, and re-layouts, on_device(): gathered[:, which_slot].astype(jnp.float32)  13 us
    gather x1, local copies, waits for them, and re-layouts, on_device(): gathered = returned_rows[place].reshape(local_tokens, TOP, model_width)  11.2 us
    scatter x1, local copies, waits for them, and re-layouts, on_device(): outgoing = jnp.zeros((experts * capacity, model_width), jnp.bfloat16).at[...  10.2 us
  transfers between devices with their start and end apart: 4, of which 3 were waited for; matrix products, arithmetic and copies ran while one was open for 1% of the time, Pallas kernels for 0%

commit v1 on v0

--- a/solution.py
+++ b/solution.py
@@ -1,6 +1,8 @@
 import jax
 import jax.numpy as jnp
 from jax import lax
+from jax.experimental import pallas as pl
+from jax.experimental.pallas import tpu as pltpu
 from jax.sharding import PartitionSpec as P
 
 HDIM = 128
@@ -36,7 +38,7 @@
     return jnp.dot(middle, down_rows, preferred_element_type=jnp.float32)
 
 
-def on_device(
+def by_slots(
     queries,
     key_rows,
     value_rows,
@@ -109,9 +111,92 @@
     return moe_sum.astype(jnp.bfloat16)
 
 
+def attention_kernel(q_ref, k_ref, v_ref, o_ref):
+    for at in range(q_ref.shape[1] // HDIM):
+        cols = slice(at * HDIM, (at + 1) * HDIM)
+        scores = lax.dot_general(
+            q_ref[:, cols],
+            k_ref[:, cols],
+            (((1,), (1,)), ((), ())),
+            preferred_element_type=jnp.float32,
+        ) * HDIM ** (-0.5)
+        exp_scores = jnp.exp(scores - jnp.max(scores, axis=-1, keepdims=True))
+        row_total = jnp.sum(exp_scores, axis=-1, keepdims=True)
+        mixed_head = jnp.dot(
+            exp_scores.astype(jnp.bfloat16), v_ref[:, cols], preferred_element_type=jnp.float32
+        )
+        o_ref[:, cols] = (mixed_head / row_total).astype(o_ref.dtype)
+
+
+def attention(queries, key_rows, value_rows):
+    rows, cols = queries.shape
+    width = 2 * HDIM
+    spec = pl.BlockSpec((rows, width), lambda h: (0, h))
+    return pl.pallas_call(
+        attention_kernel,
+        grid=(cols // width,),
+        in_specs=[spec] * 3,
+        out_specs=spec,
+        out_shape=jax.ShapeDtypeStruct((rows, cols), jnp.bfloat16),
+        cost_estimate=pl.CostEstimate(
+            flops=4 * rows * rows * cols,
+            bytes_accessed=8 * rows * cols,
+            transcendentals=rows * rows * cols // HDIM,
+        ),
+    )(queries, key_rows, value_rows)
+
+
+def hidden_and_normed(queries, key_rows, value_rows, residual, norm_gain):
+    attended = lax.all_to_all(
+        attention(queries, key_rows, value_rows), "seq", split_axis=0, concat_axis=1, tiled=True
+    )
+    hidden = (residual.astype(jnp.float32) + attended.astype(jnp.float32)).astype(jnp.bfloat16)
+    hidden_f = hidden.astype(jnp.float32)
+    mean_sq = jnp.mean(hidden_f * hidden_f, axis=-1, keepdims=True)
+    normed = (hidden_f * lax.rsqrt(mean_sq + epsilon) * norm_gain).astype(jnp.bfloat16)
+    return hidden, normed
+
+
+def own_gates(rows, ids, router_weight):
+    experts = router_weight.shape[1]
+    logits = jnp.dot(rows, router_weight, preferred_element_type=jnp.float32)
+    catalog = jnp.arange(experts, dtype=jnp.int32)
+    chosen = jnp.any(ids[:, :, None] == catalog[None, None, :], axis=1)
+    sigmoids = jnp.where(chosen, jax.nn.sigmoid(logits), 0.0)
+    gates = sigmoids / jnp.sum(sigmoids, axis=1, keepdims=True)
+    mine = catalog == lax.axis_index("exp")
+    return jnp.sum(jnp.where(mine[None, :], gates, 0.0), axis=1, keepdims=True)
+
+
+def by_rows(
+    queries,
+    key_rows,
+    value_rows,
+    residual,
+    norm_gain,
+    router_weight,
+    expert_ids,
+    gate_proj,
+    up_proj,
+    down_proj,
+):
+    ids = lax.all_gather(expert_ids, "exp", axis=0, tiled=True)
+    gate_all = lax.all_gather(gate_proj[0], "seq", axis=1, tiled=True)
+    up_all = lax.all_gather(up_proj[0], "seq", axis=1, tiled=True)
+    down_all = lax.all_gather(down_proj[0], "seq", axis=0, tiled=True)
+    hidden, normed = hidden_and_normed(queries, key_rows, value_rows, residual, norm_gain)
+    rows = lax.all_gather(normed, "exp", axis=0, tiled=True)
+    gates = own_gates(rows, ids, router_weight)
+    weighted = gates * expert_partial(rows, gate_all, up_all, down_all)
+    summed = lax.psum_scatter(
+        weighted.astype(jnp.bfloat16), "exp", scatter_dimension=0, tiled=True
+    )
+    return (hidden.astype(jnp.float32) + summed.astype(jnp.float32)).astype(jnp.bfloat16)
+
+
 def solution(mesh):
     return jax.shard_map(
-        on_device,
+        by_rows if mesh.shape["exp"] <= 8 else by_slots,
         mesh=mesh,
         in_specs=(
             P(("groups", "exp"), "seq"),

time: 451 us -> 355 us (0.79)
  blocking collectives: 129 us -> 33.9 us
  waiting for transfers between devices: 165 us -> 256 us
  local copies, waits for them, and re-layouts: 91.6 us -> 1.05 us
  starting transfers between devices: 10.7 us -> 0.16 us
  matrix products: 29.1 us -> 38 us
  Pallas kernels: 0 us -> 7.78 us
  other arithmetic: 11.3 us -> 4.17 us
    all_to_all x1, blocking collectives: 129 us -> 5.57 us  [hidden_and_normed(): lax.all_to_all(attention(queries, key_rows, value_rows), 'seq', split_axi...]
    all_to_all x2 -> x0, waiting for transfers between devices: 121 us -> none  [the longest x1 121 us: on_device(): lax.all_to_all(summed, 'exp', split_axis=0, concat_axis=0, tiled=True)]
    reduce_scatter x1, waiting for transfers between devices: 20.9 us -> 134 us  [by_rows(): lax.psum_scatter(weighted.astype(jnp.bfloat16), 'exp', scatter_dimension=...]
    all_gather x1 -> x4, waiting for transfers between devices: 22.3 us -> 120 us  [the longest x1 84.5 us: by_rows(): rows = lax.all_gather(normed, 'exp', axis=0, tiled=True)]
    all_gather x0 -> x1, blocking collectives: none -> 28.4 us  [by_rows(): ids = lax.all_gather(expert_ids, 'exp', axis=0, tiled=True)]
    unnamed x31 -> x8, local copies, waits for them, and re-layouts: 27 us -> 0.87 us
    reshape x2 -> x0, local copies, waits for them, and re-layouts: 13.7 us -> none  [the longest x1 7 us: on_device(): gathered = returned_rows[place].reshape(local_tokens, TOP, model_width)]
    dot_general x1, matrix products: 8.52 us -> 22.1 us  [expert_partial(): return jnp.dot(middle, down_rows, preferred_element_type=jnp.float32)]
  transfers between devices with their start and end apart: 4 -> 5, of which waited for: 3 -> 5; matrix products, arithmetic and copies ran while one was open for 1% -> 5% of each run, Pallas kernels for 0% -> 0%
where the time goes in v1:
time: 355 us; the launch traced here: 354 us
  waiting for transfers between devices  256 us (72%)
  matrix products  38 us (11%)
  blocking collectives  33.9 us (10%)
  between operations  13.2 us (4%)
  Pallas kernels  7.78 us (2%)
  other arithmetic  4.17 us (1%)
    reduce_scatter x1, waiting for transfers between devices, by_rows(): lax.psum_scatter(weighted.astype(jnp.bfloat16), 'exp', scatter_dimension=...  134 us
    all_gather x1, waiting for transfers between devices, by_rows(): rows = lax.all_gather(normed, 'exp', axis=0, tiled=True)  84.5 us
    all_gather x1, blocking collectives, by_rows(): ids = lax.all_gather(expert_ids, 'exp', axis=0, tiled=True)  28.4 us
    dot_general x1, matrix products, expert_partial(): return jnp.dot(middle, down_rows, preferred_element_type=jnp.float32)  22.1 us
    all_gather x1, waiting for transfers between devices, by_rows(): down_all = lax.all_gather(down_proj[0], 'seq', axis=0, tiled=True)  18.2 us
    dot_general x1, matrix products, expert_partial(): up_out = jnp.dot(row_block, up_cols, preferred_element_type=jnp.float32)  10.8 us
    all_gather x1, waiting for transfers between devices, by_rows(): up_all = lax.all_gather(up_proj[0], 'seq', axis=1, tiled=True)  10 us
    pallas_call x1, Pallas kernels, attention(): pl.pallas_call(attention_kernel, grid=(cols // width,), in_specs=[spec] *...  7.78 us
  transfers between devices with their start and end apart: 5, of which 5 were waited for; matrix products, arithmetic and copies ran while one was open for 5% of the time, Pallas kernels for 0%

profile of v1, /device:TPU:0, one launch (start us, length us, event | category | flops | bytes accessed | tf_op | source)
XLA Modules:
  0.0 354.3 jit_solution(10328169660000936660)
XLA Ops:
  6.5 0.0 copy-start
  6.5 0.0 all-gather.8.cloned.1.call-start
  6.5 7.8 %shard_map.100 = bf16[256,1792]{1,0:T(8,128)(2,1)} custom-call(bf16[256,1792]{1,0:T(8,128)(2,1)} %q_ref.1, bf16[256,1792]{1,0:T(8,128)(2,1)} %k_ref.1, bf16[256,1792]{1,0:T(8,128)(2,1)} %v_ref.1), custom_call_target="tpu_custom_call" | custom-call | flops 469762048 | bytes 3670016 | tf_op jit(solution)/shard_map/pallas_call | solution.py:135
  14.3 5.6 %all_to_all.13 = bf16[2,128,1792]{2,1,0:T(8,128)(2,1)S(1)} all-to-all(bf16[2,128,1792]{2,1,0:T(8,128)(2,1)} %bitcast.23), channel_id=1, replica_groups=mesh['groups'=2,'exp'=8,'seq'=2] {'seq'}, dimensions={0} | all-to-all | bytes 1835008 | tf_op jit(solution)/shard_map/all_to_all | solution.py:150
  19.9 0.0 copy-start.1
  19.9 0.1 convert_bitcast_fusion
  20.0 0.0 copy-start.2
  20.0 0.2 copy.14
  20.2 0.8 copy-done.1
  21.1 0.4 fusion.7
  21.4 0.0 copy-done.2
  21.4 1.2 fusion.9
  22.7 0.0 all-gather.8.cloned.1.call-update
  22.7 0.0 all-gather.12.cloned.1.call-start
  22.7 0.7 all-gather.12.cloned.1.call-update
  23.4 0.0 copy-start.3
  23.4 0.0 all-gather.10.cloned.1.call-start
  23.5 0.7 all-gather.10.cloned.1.call-update
  24.2 0.0 all-gather.14.cloned.1.call-start
  24.2 0.5 all-gather.14.cloned.1.call-update
  24.8 0.0 reduce-scatter.2.cloned.1.call-start
  24.8 0.0 copy-done.3
  24.8 28.4 %all_gather.15 = s32[1024,4]{0,1:T(4,128)S(1)} all-gather(s32[128,4]{0,1:T(4,128)S(1)} %copy-done.3), channel_id=1, replica_groups=mesh['groups'=2,'exp'=8,'seq'=2] {'exp'}, dimensions={0}, use_global_device_ids=true | all-gather | bytes 18432 | tf_op jit(solution)/shard_map/all_gather | solution.py:183
  53.2 84.5 %all-gather.8.cloned.1.call-done = bf16[1024,3584]{1,0:T(8,128)(2,1)} async-done(((bf16[128,3584]{1,0:T(8,128)(2,1)}), bf16[1024,3584]{1,0:T(8,128)(2,1)}) %all-gather.8.cloned.1.call-update) | async-done | bytes 7340048 | tf_op jit(solution)/shard_map/all_gather | solution.py:188
  137.7 0.0 copy-done
  137.7 5.1 %fusion.19 = (f32[1024]{0:T(1024)S(1)}, f32[1024,8]{0,1:T(8,128)S(1)}) fusion(pred[1024,8]{0,1:T(8,128)(4,1)S(1)} %fusion.17, bf16[1024,3584]{1,0:T(8,128)(2,1)} %all-gather.8.cloned.1.call-done, bf16[3584,8]{0,1:T(8,128)(2,1)S(1)} %copy-done), kind=kOutput, calls=%fused_computation.27 | convolution fusion | flops 58760192 | bytes 7442432 | tf_op jit(solution)/shard_map/dot_general | solution.py:162
  142.8 0.1 select_reduce_fusion
  142.9 10.0 %all-gather.12.cloned.1.call-done = bf16[1,3584,768]{2,1,0:T(8,128)(2,1)} async-done(((bf16[1,3584,384]{2,1,0:T(8,128)(2,1)}), bf16[1,3584,768]{2,1,0:T(8,128)(2,1)}) %all-gather.12.cloned.1.call-update) | async-done | bytes 5505040 | tf_op jit(solution)/shard_map/all_gather | solution.py:185
  152.9 10.8 %fusion.1 = f32[1024,768]{1,0:T(8,128)} fusion(bf16[1024,3584]{1,0:T(8,128)(2,1)} %all-gather.8.cloned.1.call-done, bf16[1,3584,768]{2,1,0:T(8,128)(2,1)} %all-gather.12.cloned.1.call-done), kind=kOutput, calls=%fused_computation.2 | convolution fusion | flops 5637144576 | bytes 15990784 | tf_op jit(solution)/shard_map/dot_general | solution.py:36
  163.8 7.4 %all-gather.10.cloned.1.call-done = bf16[1,3584,768]{2,1,0:T(8,128)(2,1)} async-done(((bf16[1,3584,384]{2,1,0:T(8,128)(2,1)}), bf16[1,3584,768]{2,1,0:T(8,128)(2,1)}) %all-gather.10.cloned.1.call-update) | async-done | bytes 5505040 | tf_op jit(solution)/shard_map/all_gather | solution.py:184
  171.1 18.2 %all-gather.14.cloned.1.call-done = bf16[1,768,3584]{2,1,0:T(8,128)(2,1)} async-done(((bf16[1,384,3584]{2,1,0:T(8,128)(2,1)}), bf16[1,768,3584]{2,1,0:T(8,128)(2,1)}) %all-gather.14.cloned.1.call-update) | async-done | bytes 5505040 | tf_op jit(solution)/shard_map/all_gather | solution.py:186
  189.3 22.1 %multiply_convert_fusion = bf16[1024,3584]{1,0:T(8,128)(2,1)} fusion(f32[1024]{0:T(1024)S(1)} %select_reduce_fusion, bf16[1,768,3584]{2,1,0:T(8,128)(2,1)} %all-gather.14.cloned.1.call-done, f32[1024,768]{1,0:T(8,128)} %fusion.1, bf16[1024,3584]{1,0:T(8,128)(2,1)} %all-gather.8.cloned.1.call-done, bf16[1,3584,768]{2,1,0:T(8,128)(2,1)} %all-gather.10.cloned.1.call-done), kind=kOutput, calls=%fused_computation | convolution fusion | flops 11286347776 | bytes 28839936 | tf_op jit(solution)/shard_map/dot_general | solution.py:38
  211.4 0.0 reduce-scatter.2.cloned.1.call-update
  211.4 134.0 %reduce-scatter.2.cloned.1.call-done = bf16[128,3584]{1,0:T(8,128)(2,1)} async-done(((bf16[1024,3584]{1,0:T(8,128)(2,1)}), bf16[128,3584]{1,0:T(8,128)(2,1)}) %reduce-scatter.2.cloned.1.call-update) | async-done | bytes 917520 | tf_op jit(solution)/shard_map/reduce_scatter | solution.py:191
  345.4 2.4 fusion.10
  (3 shorter events, 0.0 us)
Async XLA Ops:
  6.5 131.2 %copy-start = (bf16[3584,8]{0,1:T(8,128)(2,1)S(1)}, bf16[3584,8]{0,1:T(8,128)(2,1)}, u32[]{:S(2)}) copy-start(bf16[3584,8]{0,1:T(8,128)(2,1)} %param.15) | copy-start | bytes 172036
  6.5 131.2 %all-gather.8.cloned.1.call-start = ((), (), s32[]{:S(2)}) async-start(), calls=%async_computation.2 | async-start | bytes 8257536 | tf_op jit(solution)/shard_map/all_gather | solution.py:188
  19.9 1.2 copy-start.1
  20.0 1.4 copy-start.2
  22.7 130.2 %all-gather.12.cloned.1.call-start = ((), (), s32[]{:S(2)}) async-start(), calls=%async_computation.5 | async-start | bytes 8257536 | tf_op jit(solution)/shard_map/all_gather | solution.py:185
  23.4 1.4 copy-start.3
  23.4 147.7 %all-gather.10.cloned.1.call-start = ((), (), s32[]{:S(2)}) async-start(), calls=%async_computation.4 | async-start | bytes 8257536 | tf_op jit(solution)/shard_map/all_gather | solution.py:184
  24.2 165.2 %all-gather.14.cloned.1.call-start = ((), (), s32[]{:S(2)}) async-start(), calls=%async_computation.6 | async-start | bytes 8257536 | tf_op jit(solution)/shard_map/all_gather | solution.py:186
  24.8 320.7 %reduce-scatter.2.cloned.1.call-start = ((), (), s32[]{:S(2)}) async-start(), calls=%async_computation.3 | async-start | bytes 8257536 | tf_op jit(solution)/shard_map/reduce_scatter | solution.py:191
Sparse Core Ops, SparseCore 0:
  22.8 114.8 all-gather.7
  139.3 13.6 all-gather.11
  154.5 16.6 all-gather.9
  172.5 16.7 all-gather.13
  211.6 133.8 reduce-scatter.1

commit v2 on v1

--- a/solution.py
+++ b/solution.py
@@ -1,3 +1,5 @@
+import functools
+
 import jax
 import jax.numpy as jnp
 from jax import lax
@@ -157,15 +159,422 @@
     return hidden, normed
 
 
-def own_gates(rows, ids, router_weight):
+SHARED = 16
+MESH = pl.DeviceIdType.MESH
+
+
+def dense_gates(normed, ids, router_weight):
     experts = router_weight.shape[1]
-    logits = jnp.dot(rows, router_weight, preferred_element_type=jnp.float32)
+    logits = jnp.dot(normed, router_weight, preferred_element_type=jnp.float32)
     catalog = jnp.arange(experts, dtype=jnp.int32)
     chosen = jnp.any(ids[:, :, None] == catalog[None, None, :], axis=1)
     sigmoids = jnp.where(chosen, jax.nn.sigmoid(logits), 0.0)
-    gates = sigmoids / jnp.sum(sigmoids, axis=1, keepdims=True)
-    mine = catalog == lax.axis_index("exp")
-    return jnp.sum(jnp.where(mine[None, :], gates, 0.0), axis=1, keepdims=True)
+    return sigmoids / jnp.sum(sigmoids, axis=1, keepdims=True)
+
+
+def expert_kernel(
+    owners,
+    normed_ref,
+    gates_ref,
+    gate_ref,
+    up_ref,
+    down_ref,
+    out_ref,
+    rows,
+    sums,
+    from_side,
+    from_below,
+    from_above,
+    gate_all,
+    up_all,
+    down_all,
+    middle,
+    gates,
+    local_sem,
+    weight_send,
+    weight_recv,
+    gates_send,
+    gates_recv,
+    shared_sems,
+    side_send,
+    side_recv,
+    up_send,
+    down_send,
+    line_recv,
+    back_side_send,
+    back_side_recv,
+    back_up_send,
+    back_up_recv,
+    back_down_send,
+    back_down_recv,
+    last_sems,
+):
+    length = owners // 2
+    tokens, width = normed_ref.shape
+    half = gate_ref.shape[1]
+    apart = tokens - SHARED
+    me = lax.axis_index("exp")
+    core = lax.axis_index("seq")
+    z = me // 2
+    y = me % 2
+    side = {"exp": me + 1 - 2 * y}
+    other_core = {"seq": 1 - core}
+    above = {"exp": me + 2}
+    below = {"exp": me - 2}
+    has_above = z + 1 < length
+    has_below = z > 0
+
+    def start_of(count):
+        return pl.multiple_of(count, 16)
+
+    line_rows = pl.ds(start_of(y * apart), tokens + SHARED)
+    my_apart = pl.ds(start_of(y * (tokens + SHARED)), apart)
+    side_apart = pl.ds(start_of((1 - y) * (tokens + SHARED)), apart)
+    my_shared = pl.ds(start_of(apart + y * SHARED), SHARED)
+    side_shared = pl.ds(start_of(apart + (1 - y) * SHARED), SHARED)
+    own_rows = pl.ds(start_of(y * tokens), tokens)
+
+    def remote(src, dst, send, recv, device):
+        return pltpu.make_async_remote_copy(
+            src_ref=src, dst_ref=dst, send_sem=send, recv_sem=recv, device_id=device, device_id_type=MESH
+        )
+
+    def own_weights(at):
+        src = (gate_ref, up_ref, down_ref)[at]
+        dst = (
+            gate_all.at[:, pl.ds(0, half)],
+            up_all.at[:, pl.ds(0, half)],
+            down_all.at[pl.ds(0, half)],
+        )[at]
+        return pltpu.make_async_copy(src, dst, local_sem.at[at])
+
+    def other_weights(at):
+        src = (gate_ref, up_ref, down_ref)[at]
+        dst = (
+            gate_all.at[:, pl.ds(half, half)],
+            up_all.at[:, pl.ds(half, half)],
+            down_all.at[pl.ds(half, half)],
+        )[at]
+        return remote(src, dst, weight_send.at[at], weight_recv.at[at], other_core)
+
+    def gates_copy(step):
+        to = lax.rem(me + step, owners)
+        return remote(
+            gates_ref, gates.at[me], gates_send.at[step], gates_recv.at[step], {"exp": to}
+        )
+
+    def shared_copy():
+        return remote(
+            rows.at[z, my_shared], rows.at[z, my_shared], shared_sems.at[0], shared_sems.at[1], side
+        )
+
+    def side_copy(at):
+        return remote(
+            rows.at[at, my_apart], rows.at[at, my_apart], side_send.at[at], side_recv.at[at], side
+        )
+
+    def up_copy(at):
+        return remote(
+            rows.at[at, line_rows], rows.at[at, line_rows], up_send.at[at], line_recv.at[at], above
+        )
+
+    def down_copy(at):
+        return remote(
+            rows.at[at, line_rows], rows.at[at, line_rows], down_send.at[at], line_recv.at[at], below
+        )
+
+    def back_side_copy(at):
+        return remote(
+            sums.at[at, side_apart],
+            from_side.at[at],
+            back_side_send.at[at],
+            back_side_recv.at[at],
+            side,
+        )
+
+    def back_up_copy(at):
+        return remote(
+            sums.at[at, line_rows],
+            from_below.at[at],
+            back_up_send.at[at],
+            back_up_recv.at[at],
+            above,
+        )
+
+    def back_down_copy(at):
+        return remote(
+            sums.at[at, line_rows],
+            from_above.at[at],
+            back_down_send.at[at],
+            back_down_recv.at[at],
+            below,
+        )
+
+    def last_copy():
+        return remote(
+            sums.at[z, side_shared],
+            from_side.at[length, pl.ds(0, SHARED)],
+            last_sems.at[0],
+            last_sems.at[1],
+            side,
+        )
+
+    barrier = pltpu.get_barrier_semaphore()
+    for step in range(1, owners):
+        pl.semaphore_signal(
+            barrier, inc=1, device_id={"exp": lax.rem(me + step, owners)}, device_id_type=MESH
+        )
+    pl.semaphore_signal(barrier, inc=1, device_id=other_core, device_id_type=MESH)
+    own_copy = pltpu.make_async_copy(normed_ref, rows.at[z, own_rows], local_sem.at[3])
+    own_copy.start()
+    own_gates = pltpu.make_async_copy(gates_ref, gates.at[me], local_sem.at[4])
+    own_gates.start()
+    own_copy.wait()
+    pl.semaphore_wait(barrier, owners)
+
+    shared_copy().start()
+    side_copy(z).start()
+    for step in range(1, owners):
+        gates_copy(step).start()
+    for at in range(3):
+        other_weights(at).start()
+    for at in range(3):
+        own_weights(at).start()
+    shared_copy().wait_recv()
+
+    @pl.when(has_above)
+    def _():
+        up_copy(z).start()
+
+    @pl.when(has_below)
+    def _():
+        down_copy(z).start()
+
+    own_gates.wait()
+    for step in range(1, owners):
+        gates_copy(step).wait_recv()
+    for at in range(3):
+        own_weights(at).wait()
+        other_weights(at).wait_recv()
+
+    def expert_sums(at):
+        grid_row = lax.broadcasted_iota(jnp.int32, (tokens, tokens), 0)
+        grid_col = lax.broadcasted_iota(jnp.int32, (tokens, tokens), 1)
+
+        def gate_column(which):
+            table = gates[2 * at + which]
+            mine = lax.broadcasted_iota(jnp.int32, table.shape, 0) == me
+            line = jnp.sum(jnp.where(mine, table, 0.0), axis=0, keepdims=True)
+            return jnp.sum(jnp.where(grid_row == grid_col, line, 0.0), axis=1, keepdims=True)
+
+        gate_col = jnp.concatenate([gate_column(0), gate_column(1)], axis=0)
+
+        def middle_tile(tile, carry):
+            cols = pl.ds(pl.multiple_of(tile * 256, 256), 256)
+            gate_out = jnp.dot(rows[at], gate_all[:, cols], preferred_element_type=jnp.float32)
+            up_out = jnp.dot(rows[at], up_all[:, cols], preferred_element_type=jnp.float32)
+            middle[:, cols] = (gate_out / (1.0 + jnp.exp(-gate_out)) * up_out).astype(jnp.bfloat16)
+            return carry
+
+        lax.fori_loop(0, 2 * half // 256, middle_tile, 0)
+
+        def out_tile(tile, carry):
+            cols = pl.ds(pl.multiple_of(tile * 512, 512), 512)
+            part = jnp.dot(middle[...], down_all[:, cols], preferred_element_type=jnp.float32)
+            sums[at, :, cols] = (part * gate_col).astype(jnp.bfloat16)
+            return carry
+
+        lax.fori_loop(0, width // 512, out_tile, 0)
+
+    def place(step):
+        away = (step + 1) // 2
+        return jnp.where(step % 2 == 1, z - away, z + away)
+
+    def inside(at):
+        return jnp.logical_and(at >= 0, at < length)
+
+    def gather_step(step):
+        at = place(step)
+
+        @pl.when(inside(at))
+        def _():
+            up_copy(at).wait_recv()
+
+            @pl.when(jnp.logical_and(at < z, has_above))
+            def _():
+                up_copy(at).start()
+
+            @pl.when(jnp.logical_and(at > z, has_below))
+            def _():
+                down_copy(at).start()
+
+            side_copy(at).start()
+
+    def compute_step(step):
+        at = place(step)
+
+        @pl.when(inside(at))
+        def _():
+            side_copy(at).wait_recv()
+            expert_sums(at)
+            back_side_copy(at).start()
+
+    steps = 2 * length - 1
+
+    def gather_and_compute(step, carry):
+        @pl.when(jnp.logical_and(step >= 1, step < steps))
+        def _():
+            gather_step(step)
+
+        @pl.when(step >= 2)
+        def _():
+            compute_step(step - 2)
+
+        return carry
+
+    lax.fori_loop(0, steps + 2, gather_and_compute, 0)
+
+    def add_rows(at, first, source, first_source, count):
+        def add_some(piece, carry):
+            into = pl.ds(start_of(first + piece * 16), 16)
+            what = pl.ds(start_of(first_source + piece * 16), 16)
+            sums[at, into] = (
+                sums[at, into].astype(jnp.float32) + source[at, what].astype(jnp.float32)
+            ).astype(jnp.bfloat16)
+            return carry
+
+        lax.fori_loop(0, count // 16, add_some, 0)
+
+    def add_side(at):
+        back_side_copy(at).wait_recv()
+        add_rows(at, y * (tokens + SHARED), from_side, 0, apart)
+
+    def add_below(at):
+        back_up_copy(at).wait_recv()
+        add_rows(at, y * apart, from_below, 0, tokens + SHARED)
+
+    def add_above(at):
+        back_down_copy(at).wait_recv()
+        add_rows(at, y * apart, from_above, 0, tokens + SHARED)
+
+    def return_step(step, carry):
+        high = length - 1 - step
+
+        @pl.when(high > z)
+        def _():
+            add_side(high)
+
+            @pl.when(has_below)
+            def _():
+                add_below(high)
+
+            back_up_copy(high).start()
+
+        @pl.when(step < z)
+        def _():
+            add_side(step)
+
+            @pl.when(has_above)
+            def _():
+                add_above(step)
+
+            back_down_copy(step).start()
+
+        return carry
+
+    lax.fori_loop(0, length - 1, return_step, 0)
+    add_side(z)
+
+    @pl.when(has_below)
+    def _():
+        add_below(z)
+
+    @pl.when(has_above)
+    def _():
+        add_above(z)
+
+    last_copy().start()
+    out_ref[...] = sums[z, own_rows]
+    last_copy().wait_recv()
+    out_shared = pl.ds(start_of((1 - y) * apart), SHARED)
+    out_ref[out_shared] = (
+        out_ref[out_shared].astype(jnp.float32)
+        + from_side[length, pl.ds(0, SHARED)].astype(jnp.float32)
+    ).astype(jnp.bfloat16)
+
+    last_copy().wait_send()
+    shared_copy().wait_send()
+    for step in range(1, owners):
+        gates_copy(step).wait_send()
+    for at in range(3):
+        other_weights(at).wait_send()
+
+    def drain(at, carry):
+        side_copy(at).wait_send()
+        back_side_copy(at).wait_send()
+
+        @pl.when(jnp.logical_and(at <= z, has_above))
+        def _():
+            up_copy(at).wait_send()
+
+        @pl.when(jnp.logical_and(at >= z, has_below))
+        def _():
+            down_copy(at).wait_send()
+
+        @pl.when(at > z)
+        def _():
+            back_up_copy(at).wait_send()
+
+        @pl.when(at < z)
+        def _():
+            back_down_copy(at).wait_send()
+
+        return carry
+
+    lax.fori_loop(0, length, drain, 0)
+
+
+def routed_experts(normed, gates, gate_half, up_half, down_half):
+    tokens, width = normed.shape
+    owners = gates.shape[0]
+    length = owners // 2
+    half = gate_half.shape[1]
+    anywhere = pl.BlockSpec(memory_space=pl.ANY)
+    dma = pltpu.SemaphoreType.DMA
+    return pl.pallas_call(
+        functools.partial(expert_kernel, owners),
+        in_specs=[anywhere] * 5,
+        out_specs=pl.BlockSpec(memory_space=pltpu.VMEM),
+        out_shape=jax.ShapeDtypeStruct((tokens, width), jnp.bfloat16),
+        scratch_shapes=[
+            pltpu.VMEM((length, 2 * tokens, width), jnp.bfloat16),
+            pltpu.VMEM((length, 2 * tokens, width), jnp.bfloat16),
+            pltpu.VMEM((length + 1, tokens - SHARED, width), jnp.bfloat16),
+            pltpu.VMEM((length, tokens + SHARED, width), jnp.bfloat16),
+            pltpu.VMEM((length, tokens + SHARED, width), jnp.bfloat16),
+            pltpu.VMEM((width, 2 * half), jnp.bfloat16),
+            pltpu.VMEM((width, 2 * half), jnp.bfloat16),
+            pltpu.VMEM((2 * half, width), jnp.bfloat16),
+            pltpu.VMEM((2 * tokens, 2 * half), jnp.bfloat16),
+            pltpu.VMEM((owners, owners, tokens), jnp.float32),
+            dma((5,)),
+            dma((3,)),
+            dma((3,)),
+            dma((owners,)),
+            dma((owners,)),
+            dma((2,)),
+        ]
+        + [dma((length,))] * 11
+        + [dma((2,))],
+        compiler_params=pltpu.CompilerParams(
+            collective_id=0, has_side_effects=True, vmem_limit_bytes=58 * 1024 * 1024
+        ),
+        cost_estimate=pl.CostEstimate(
+            flops=12 * owners * tokens * width * half,
+            bytes_accessed=12 * width * half,
+            transcendentals=2 * owners * tokens * half,
+        ),
+    )(normed, gates, gate_half, up_half, down_half)
 
 
 def by_rows(
@@ -180,23 +589,15 @@
     up_proj,
     down_proj,
 ):
-    ids = lax.all_gather(expert_ids, "exp", axis=0, tiled=True)
-    gate_all = lax.all_gather(gate_proj[0], "seq", axis=1, tiled=True)
-    up_all = lax.all_gather(up_proj[0], "seq", axis=1, tiled=True)
-    down_all = lax.all_gather(down_proj[0], "seq", axis=0, tiled=True)
     hidden, normed = hidden_and_normed(queries, key_rows, value_rows, residual, norm_gain)
-    rows = lax.all_gather(normed, "exp", axis=0, tiled=True)
-    gates = own_gates(rows, ids, router_weight)
-    weighted = gates * expert_partial(rows, gate_all, up_all, down_all)
-    summed = lax.psum_scatter(
-        weighted.astype(jnp.bfloat16), "exp", scatter_dimension=0, tiled=True
-    )
+    gates = jnp.transpose(dense_gates(normed, expert_ids, router_weight))
+    summed = routed_experts(normed, gates, gate_proj[0], up_proj[0], down_proj[0])
     return (hidden.astype(jnp.float32) + summed.astype(jnp.float32)).astype(jnp.bfloat16)
 
 
 def solution(mesh):
     return jax.shard_map(
-        by_rows if mesh.shape["exp"] <= 8 else by_slots,
+        by_rows if mesh.shape["exp"] == 8 else by_slots,
         mesh=mesh,
         in_specs=(
             P(("groups", "exp"), "seq"),

time: 355 us -> 260 us (0.73)
  waiting for transfers between devices: 256 us -> 0 us
  Pallas kernels: 7.78 us -> 248 us
  matrix products: 38 us -> 0.36 us
  blocking collectives: 33.9 us -> 5.57 us
  between operations: 13.2 us -> 0.07 us
    pallas_call x0 -> x1, Pallas kernels: none -> 241 us  [routed_experts(): pl.pallas_call(functools.partial(expert_kernel, owners), in_specs=[anywhe...]
    reduce_scatter x1 -> x0, waiting for transfers between devices: 134 us -> none  [by_rows(): lax.psum_scatter(weighted.astype(jnp.bfloat16), 'exp', scatter_dimension=...]
    all_gather x4 -> x0, waiting for transfers between devices: 120 us -> none  [the longest x1 84.5 us: by_rows(): rows = lax.all_gather(normed, 'exp', axis=0, tiled=True)]
    dot_general x3 -> x1, matrix products: 38 us -> 0.36 us  [dense_gates(): logits = jnp.dot(normed, router_weight, preferred_element_type=jnp.float32)]
    all_gather x1 -> x0, blocking collectives: 28.4 us -> none  [by_rows(): ids = lax.all_gather(expert_ids, 'exp', axis=0, tiled=True)]
  transfers between devices with their start and end apart: 5 -> 0, of which waited for: 5 -> 0; matrix products, arithmetic and copies ran while one was open for 5% -> 0% of each run, Pallas kernels for 0% -> 0%
where the time goes in v2:
time: 260 us
  Pallas kernels  248 us (95%)
  blocking collectives  5.57 us (2%)
  other arithmetic  3.76 us (1%)
    pallas_call x1, Pallas kernels, routed_experts(): pl.pallas_call(functools.partial(expert_kernel, owners), in_specs=[anywhe...  241 us
    pallas_call x1, Pallas kernels, attention(): pl.pallas_call(attention_kernel, grid=(cols // width,), in_specs=[spec] *...  7.78 us
    all_to_all x1, blocking collectives, hidden_and_normed(): lax.all_to_all(attention(queries, key_rows, value_rows), 'seq', split_axi...  5.57 us

profile of v2, /device:TPU:0, one launch (start us, length us, event | category | flops | bytes accessed | tf_op | source)
XLA Modules:
  0.0 259.8 jit_solution(10095298396624268113)
XLA Ops:
  0.0 0.0 copy-start
  0.0 7.8 %shard_map.100 = bf16[256,1792]{1,0:T(8,128)(2,1)} custom-call(bf16[256,1792]{1,0:T(8,128)(2,1)} %q_ref.1, bf16[256,1792]{1,0:T(8,128)(2,1)} %k_ref.1, bf16[256,1792]{1,0:T(8,128)(2,1)} %v_ref.1), custom_call_target="tpu_custom_call" | custom-call | flops 469762048 | bytes 3670016 | tf_op jit(solution)/shard_map/pallas_call | solution.py:137
  7.8 5.6 %all_to_all.13 = bf16[2,128,1792]{2,1,0:T(8,128)(2,1)S(1)} all-to-all(bf16[2,128,1792]{2,1,0:T(8,128)(2,1)} %bitcast.13), channel_id=1, replica_groups=mesh['groups'=2,'exp'=8,'seq'=2] {'seq'}, dimensions={0} | all-to-all | bytes 1835008 | tf_op jit(solution)/shard_map/all_to_all | solution.py:152
  13.3 0.1 convert_bitcast_fusion
  13.5 0.0 copy-start.2
  13.5 0.2 copy.16
  13.7 1.0 copy-done.2
  14.7 0.0 copy-start.4
  14.7 0.0 copy-start.3
  14.7 0.4 fusion
  15.0 0.3 copy-done.4
  15.3 0.0 copy-done.3
  15.4 0.3 fusion.2.normed_ref
  15.7 0.0 copy-done
  15.7 0.0 copy-start.1
  15.7 0.4 fusion.9
  16.1 0.6 divide_bitcast_fusion.gates_ref
  16.7 0.0 copy-done.1
  16.7 240.7 %shard_map.101 = bf16[128,3584]{1,0:T(8,128)(2,1)} custom-call(bf16[128,3584]{1,0:T(8,128)(2,1)} %copy-done.1, f32[8,128]{1,0:T(8,128)} %divide_bitcast_fusion.gates_ref, bf16[3584,384]{1,0:T(8,128)(2,1)} %bitcast.14, bf16[3584,384]{1,0:T(8,128)(2,1)} %bitcast.15, bf16[384,3584]{1,0:T(8,128)(2,1)} %bitcast.16), custom_call_target="tpu_custom_call" | custom-call | flops 16911433728 | bytes 16515072 | tf_op jit(solution)/shard_map/pallas_call | solution.py:544
  257.4 2.4 fusion.3
  (2 shorter events, 0.0 us)
Async XLA Ops:
  0.0 15.7 %copy-start = (bf16[3584,8]{0,1:T(8,128)(2,1)S(1)}, bf16[3584,8]{0,1:T(8,128)(2,1)}, u32[]{:S(2)}) copy-start(bf16[3584,8]{0,1:T(8,128)(2,1)} %param.15) | copy-start | bytes 172036
  13.5 1.2 copy-start.2
  14.7 0.7 copy-start.4
  14.7 0.7 copy-start.3
  15.7 1.0 copy-start.1

commit v3 on v2

--- a/solution.py
+++ b/solution.py
@@ -159,7 +159,8 @@
     return hidden, normed
 
 
-SHARED = 16
+SHARED = 48
+PIECES = 4
 MESH = pl.DeviceIdType.MESH
 
 
@@ -195,7 +196,8 @@
     weight_recv,
     gates_send,
     gates_recv,
-    shared_sems,
+    shared_send,
+    shared_recv,
     side_send,
     side_recv,
     up_send,
@@ -207,7 +209,8 @@
     back_up_recv,
     back_down_send,
     back_down_recv,
-    last_sems,
+    last_send,
+    last_recv,
 ):
     length = owners // 2
     tokens, width = normed_ref.shape
@@ -263,59 +266,66 @@
             gates_ref, gates.at[me], gates_send.at[step], gates_recv.at[step], {"exp": to}
         )
 
-    def shared_copy():
+    piece_width = width // PIECES
+
+    def columns(piece):
+        return pl.ds(pl.multiple_of(piece * piece_width, 128), piece_width)
+
+    def shared_copy(piece):
+        block = rows.at[z, my_shared, columns(piece)]
+        return remote(block, block, shared_send.at[piece], shared_recv.at[piece], side)
+
+    def side_copy(at, piece):
+        which = at * PIECES + piece
+        block = rows.at[at, my_apart, columns(piece)]
+        return remote(block, block, side_send.at[which], side_recv.at[which], side)
+
+    def up_copy(at, piece):
+        which = at * PIECES + piece
+        block = rows.at[at, line_rows, columns(piece)]
+        return remote(block, block, up_send.at[which], line_recv.at[which], above)
+
+    def down_copy(at, piece):
+        which = at * PIECES + piece
+        block = rows.at[at, line_rows, columns(piece)]
+        return remote(block, block, down_send.at[which], line_recv.at[which], below)
+
+    def back_side_copy(at, piece):
+        which = at * PIECES + piece
         return remote(
-            rows.at[z, my_shared], rows.at[z, my_shared], shared_sems.at[0], shared_sems.at[1], side
-        )
-
-    def side_copy(at):
+            sums.at[at, side_apart, columns(piece)],
+            from_side.at[at, :, columns(piece)],
+            back_side_send.at[which],
+            back_side_recv.at[which],
+            side,
+        )
+
+    def back_up_copy(at, piece):
+        which = at * PIECES + piece
         return remote(
-            rows.at[at, my_apart], rows.at[at, my_apart], side_send.at[at], side_recv.at[at], side
-        )
-
-    def up_copy(at):
+            sums.at[at, line_rows, columns(piece)],
+            from_below.at[at, :, columns(piece)],
+            back_up_send.at[which],
+            back_up_recv.at[which],
+            above,
+        )
+
+    def back_down_copy(at, piece):
+        which = at * PIECES + piece
         return remote(
-            rows.at[at, line_rows], rows.at[at, line_rows], up_send.at[at], line_recv.at[at], above
-        )
-
-    def down_copy(at):
+            sums.at[at, line_rows, columns(piece)],
+            from_above.at[at, :, columns(piece)],
+            back_down_send.at[which],
+            back_down_recv.at[which],
+            below,
+        )
+
+    def last_copy(piece):
         return remote(
-            rows.at[at, line_rows], rows.at[at, line_rows], down_send.at[at], line_recv.at[at], below
-        )
-
-    def back_side_copy(at):
-        return remote(
-            sums.at[at, side_apart],
-            from_side.at[at],
-            back_side_send.at[at],
-            back_side_recv.at[at],
-            side,
-        )
-
-    def back_up_copy(at):
-        return remote(
-            sums.at[at, line_rows],
-            from_below.at[at],
-            back_up_send.at[at],
-            back_up_recv.at[at],
-            above,
-        )
-
-    def back_down_copy(at):
-        return remote(
-            sums.at[at, line_rows],
-            from_above.at[at],
-            back_down_send.at[at],
-            back_down_recv.at[at],
-            below,
-        )
-
-    def last_copy():
-        return remote(
-            sums.at[z, side_shared],
-            from_side.at[length, pl.ds(0, SHARED)],
-            last_sems.at[0],
-            last_sems.at[1],
+            sums.at[z, side_shared, columns(piece)],
+            from_side.at[length, pl.ds(0, SHARED), columns(piece)],
+            last_send.at[piece],
+            last_recv.at[piece],
             side,
         )
 
@@ -332,24 +342,31 @@
     own_copy.wait()
     pl.semaphore_wait(barrier, owners)
 
-    shared_copy().start()
-    side_copy(z).start()
+    for piece in range(PIECES):
+        shared_copy(piece).start()
+    for piece in range(PIECES):
+        side_copy(z, piece).start()
     for step in range(1, owners):
         gates_copy(step).start()
     for at in range(3):
         other_weights(at).start()
     for at in range(3):
         own_weights(at).start()
-    shared_copy().wait_recv()
-
-    @pl.when(has_above)
-    def _():
-        up_copy(z).start()
-
-    @pl.when(has_below)
-    def _():
-        down_copy(z).start()
-
+
+    def line_start(piece, carry):
+        shared_copy(piece).wait_recv()
+
+        @pl.when(has_above)
+        def _():
+            up_copy(z, piece).start()
+
+        @pl.when(has_below)
+        def _():
+            down_copy(z, piece).start()
+
+        return carry
+
+    lax.fori_loop(0, PIECES, line_start, 0)
     own_gates.wait()
     for step in range(1, owners):
         gates_copy(step).wait_recv()
@@ -386,152 +403,182 @@
 
         lax.fori_loop(0, width // 512, out_tile, 0)
 
-    def place(step):
-        away = (step + 1) // 2
-        return jnp.where(step % 2 == 1, z - away, z + away)
-
     def inside(at):
         return jnp.logical_and(at >= 0, at < length)
 
-    def gather_step(step):
-        at = place(step)
-
+    def gather_piece(at, piece):
         @pl.when(inside(at))
         def _():
-            up_copy(at).wait_recv()
+            up_copy(at, piece).wait_recv()
 
             @pl.when(jnp.logical_and(at < z, has_above))
             def _():
-                up_copy(at).start()
+                up_copy(at, piece).start()
 
             @pl.when(jnp.logical_and(at > z, has_below))
             def _():
-                down_copy(at).start()
-
-            side_copy(at).start()
-
-    def compute_step(step):
-        at = place(step)
-
-        @pl.when(inside(at))
-        def _():
-            side_copy(at).wait_recv()
-            expert_sums(at)
-            back_side_copy(at).start()
-
-    steps = 2 * length - 1
-
-    def gather_and_compute(step, carry):
-        @pl.when(jnp.logical_and(step >= 1, step < steps))
-        def _():
-            gather_step(step)
-
-        @pl.when(step >= 2)
-        def _():
-            compute_step(step - 2)
-
-        return carry
-
-    lax.fori_loop(0, steps + 2, gather_and_compute, 0)
-
-    def add_rows(at, first, source, first_source, count):
-        def add_some(piece, carry):
-            into = pl.ds(start_of(first + piece * 16), 16)
-            what = pl.ds(start_of(first_source + piece * 16), 16)
-            sums[at, into] = (
-                sums[at, into].astype(jnp.float32) + source[at, what].astype(jnp.float32)
+                down_copy(at, piece).start()
+
+            side_copy(at, piece).start()
+
+    def compute_block(at):
+        def wait_piece(piece, carry):
+            side_copy(at, piece).wait_recv()
+            return carry
+
+        def send_piece(piece, carry):
+            back_side_copy(at, piece).start()
+            return carry
+
+        lax.fori_loop(0, PIECES, wait_piece, 0)
+        expert_sums(at)
+        lax.fori_loop(0, PIECES, send_piece, 0)
+
+    def add_rows(at, piece, first, source, count):
+        def add_some(group, carry):
+            into = pl.ds(start_of(first + group * 16), 16)
+            what = pl.ds(start_of(group * 16), 16)
+            cols = columns(piece)
+            sums[at, into, cols] = (
+                sums[at, into, cols].astype(jnp.float32) + source[at, what, cols].astype(jnp.float32)
             ).astype(jnp.bfloat16)
             return carry
 
         lax.fori_loop(0, count // 16, add_some, 0)
 
-    def add_side(at):
-        back_side_copy(at).wait_recv()
-        add_rows(at, y * (tokens + SHARED), from_side, 0, apart)
-
-    def add_below(at):
-        back_up_copy(at).wait_recv()
-        add_rows(at, y * apart, from_below, 0, tokens + SHARED)
-
-    def add_above(at):
-        back_down_copy(at).wait_recv()
-        add_rows(at, y * apart, from_above, 0, tokens + SHARED)
-
-    def return_step(step, carry):
-        high = length - 1 - step
-
-        @pl.when(high > z)
-        def _():
-            add_side(high)
+    def add_side(at, piece):
+        back_side_copy(at, piece).wait_recv()
+        add_rows(at, piece, y * (tokens + SHARED), from_side, apart)
+
+    def add_below(at, piece):
+        back_up_copy(at, piece).wait_recv()
+        add_rows(at, piece, y * apart, from_below, tokens + SHARED)
+
+    def add_above(at, piece):
+        back_down_copy(at, piece).wait_recv()
+        add_rows(at, piece, y * apart, from_above, tokens + SHARED)
+
+    def return_up(at, piece, here):
+        @pl.when(jnp.logical_and(here, jnp.logical_and(at > z, inside(at))))
+        def _():
+            add_side(at, piece)
 
             @pl.when(has_below)
             def _():
-                add_below(high)
-
-            back_up_copy(high).start()
-
-        @pl.when(step < z)
-        def _():
-            add_side(step)
+                add_below(at, piece)
+
+            back_up_copy(at, piece).start()
+
+    def return_down(at, piece, here):
+        @pl.when(jnp.logical_and(here, jnp.logical_and(at < z, inside(at))))
+        def _():
+            add_side(at, piece)
 
             @pl.when(has_above)
             def _():
-                add_above(step)
-
-            back_down_copy(step).start()
+                add_above(at, piece)
+
+            back_down_copy(at, piece).start()
+
+    low_half = z < length // 2
+
+    def one_round(away, carry):
+        @pl.when(away < length)
+        def _():
+            def both_pieces(piece, inner):
+                gather_piece(z - away, piece)
+                gather_piece(z + away, piece)
+                return inner
+
+            lax.fori_loop(0, PIECES, both_pieces, 0)
+
+        def near_block(which, inner):
+            at = jnp.where(which == 0, z - away + 1, z + away - 1)
+
+            @pl.when(jnp.logical_and(inside(at), jnp.logical_or(which == 0, away > 1)))
+            def _():
+                compute_block(at)
+
+            return inner
+
+        lax.fori_loop(0, 2, near_block, 0)
+
+        def return_piece(piece, inner):
+            far = away - 2
+            return_up(far, piece, low_half)
+            return_down(length - 1 - far, piece, True)
+            return_up(far, piece, jnp.logical_not(low_half))
+            return inner
+
+        @pl.when(away > 2)
+        def _():
+            lax.fori_loop(0, PIECES, return_piece, 0)
 
         return carry
 
-    lax.fori_loop(0, length - 1, return_step, 0)
-    add_side(z)
-
-    @pl.when(has_below)
-    def _():
-        add_below(z)
-
-    @pl.when(has_above)
-    def _():
-        add_above(z)
-
-    last_copy().start()
-    out_ref[...] = sums[z, own_rows]
-    last_copy().wait_recv()
+    lax.fori_loop(1, length + 2, one_round, 0)
+
+    def finish_piece(piece, carry):
+        add_side(z, piece)
+
+        @pl.when(has_below)
+        def _():
+            add_below(z, piece)
+
+        @pl.when(has_above)
+        def _():
+            add_above(z, piece)
+
+        last_copy(piece).start()
+        out_ref[:, columns(piece)] = sums[z, own_rows, columns(piece)]
+        return carry
+
+    lax.fori_loop(0, PIECES, finish_piece, 0)
     out_shared = pl.ds(start_of((1 - y) * apart), SHARED)
-    out_ref[out_shared] = (
-        out_ref[out_shared].astype(jnp.float32)
-        + from_side[length, pl.ds(0, SHARED)].astype(jnp.float32)
-    ).astype(jnp.bfloat16)
-
-    last_copy().wait_send()
-    shared_copy().wait_send()
+
+    def last_piece(piece, carry):
+        last_copy(piece).wait_recv()
+        cols = columns(piece)
+        out_ref[out_shared, cols] = (
+            out_ref[out_shared, cols].astype(jnp.float32)
+            + from_side[length, pl.ds(0, SHARED), cols].astype(jnp.float32)
+        ).astype(jnp.bfloat16)
+        return carry
+
+    lax.fori_loop(0, PIECES, last_piece, 0)
+    for piece in range(PIECES):
+        last_copy(piece).wait_send()
+        shared_copy(piece).wait_send()
     for step in range(1, owners):
         gates_copy(step).wait_send()
     for at in range(3):
         other_weights(at).wait_send()
 
-    def drain(at, carry):
-        side_copy(at).wait_send()
-        back_side_copy(at).wait_send()
+    def drain(which, carry):
+        at = which // PIECES
+        piece = which % PIECES
+        side_copy(at, piece).wait_send()
+        back_side_copy(at, piece).wait_send()
 
         @pl.when(jnp.logical_and(at <= z, has_above))
         def _():
-            up_copy(at).wait_send()
+            up_copy(at, piece).wait_send()
 
         @pl.when(jnp.logical_and(at >= z, has_below))
         def _():
-            down_copy(at).wait_send()
+            down_copy(at, piece).wait_send()
 
         @pl.when(at > z)
         def _():
-            back_up_copy(at).wait_send()
+            back_up_copy(at, piece).wait_send()
 
         @pl.when(at < z)
         def _():
-            back_down_copy(at).wait_send()
+            back_down_copy(at, piece).wait_send()
 
         return carry
 
-    lax.fori_loop(0, length, drain, 0)
+    lax.fori_loop(0, length * PIECES, drain, 0)
 
 
 def routed_experts(normed, gates, gate_half, up_half, down_half):
@@ -562,10 +609,11 @@
             dma((3,)),
             dma((owners,)),
             dma((owners,)),
-            dma((2,)),
+            dma((PIECES,)),
+            dma((PIECES,)),
         ]
-        + [dma((length,))] * 11
-        + [dma((2,))],
+        + [dma((length * PIECES,))] * 11
+        + [dma((PIECES,))] * 2,
         compiler_params=pltpu.CompilerParams(
             collective_id=0, has_side_effects=True, vmem_limit_bytes=58 * 1024 * 1024
         ),

time: 260 us -> 225 us (0.87)
  Pallas kernels: 248 us -> 213 us
    pallas_call x1, Pallas kernels: 241 us -> 205 us  [routed_experts(): pl.pallas_call(functools.partial(expert_kernel, owners), in_specs=[anywhe...]
where the time goes in v3:
time: 225 us; the launch traced here: 224 us
  Pallas kernels  213 us (95%)
  blocking collectives  5.57 us (2%)
  other arithmetic  3.76 us (2%)
    pallas_call x1, Pallas kernels, routed_experts(): pl.pallas_call(functools.partial(expert_kernel, owners), in_specs=[anywhe...  205 us
    pallas_call x1, Pallas kernels, attention(): pl.pallas_call(attention_kernel, grid=(cols // width,), in_specs=[spec] *...  7.78 us
    all_to_all x1, blocking collectives, hidden_and_normed(): lax.all_to_all(attention(queries, key_rows, value_rows), 'seq', split_axi...  5.57 us

profile of v3, /device:TPU:0, one launch (start us, length us, event | category | flops | bytes accessed | tf_op | source)
XLA Modules:
  0.0 224.5 jit_solution(11958894085487954600)
XLA Ops:
  0.0 0.0 copy-start
  0.0 7.8 %shard_map.100 = bf16[256,1792]{1,0:T(8,128)(2,1)} custom-call(bf16[256,1792]{1,0:T(8,128)(2,1)} %q_ref.1, bf16[256,1792]{1,0:T(8,128)(2,1)} %k_ref.1, bf16[256,1792]{1,0:T(8,128)(2,1)} %v_ref.1), custom_call_target="tpu_custom_call" | custom-call | flops 469762048 | bytes 3670016 | tf_op jit(solution)/shard_map/pallas_call | solution.py:137
  7.8 5.6 %all_to_all.13 = bf16[2,128,1792]{2,1,0:T(8,128)(2,1)S(1)} all-to-all(bf16[2,128,1792]{2,1,0:T(8,128)(2,1)} %bitcast.13), channel_id=1, replica_groups=mesh['groups'=2,'exp'=8,'seq'=2] {'seq'}, dimensions={0} | all-to-all | bytes 1835008 | tf_op jit(solution)/shard_map/all_to_all | solution.py:152
  13.3 0.1 convert_bitcast_fusion
  13.5 0.0 copy-start.2
  13.5 0.2 copy.16
  13.7 1.0 copy-done.2
  14.7 0.0 copy-start.4
  14.7 0.0 copy-start.3
  14.7 0.4 fusion
  15.0 0.3 copy-done.4
  15.3 0.0 copy-done.3
  15.4 0.3 fusion.2.normed_ref
  15.7 0.0 copy-done
  15.7 0.0 copy-start.1
  15.7 0.4 fusion.9
  16.1 0.6 divide_bitcast_fusion.gates_ref
  16.7 0.0 copy-done.1
  16.7 205.4 %shard_map.101 = bf16[128,3584]{1,0:T(8,128)(2,1)} custom-call(bf16[128,3584]{1,0:T(8,128)(2,1)} %copy-done.1, f32[8,128]{1,0:T(8,128)} %divide_bitcast_fusion.gates_ref, bf16[3584,384]{1,0:T(8,128)(2,1)} %bitcast.14, bf16[3584,384]{1,0:T(8,128)(2,1)} %bitcast.15, bf16[384,3584]{1,0:T(8,128)(2,1)} %bitcast.16), custom_call_target="tpu_custom_call" | custom-call | flops 16911433728 | bytes 16515072 | tf_op jit(solution)/shard_map/pallas_call | solution.py:591
  222.1 2.4 %fusion.3 = bf16[128,3584]{1,0:T(8,128)(2,1)} fusion(bf16[128,3584]{1,0:T(8,128)(2,1)S(1)} %get-tuple-element.6, bf16[128,3584]{1,0:T(8,128)(2,1)} %shard_map.101), kind=kLoop, calls=%fused_computation.6 | loop fusion | flops 1835008 | bytes 2752512 | tf_op jit(solution)/shard_map/convert_element_type | solution.py:643
  (2 shorter events, 0.0 us)
Async XLA Ops:
  0.0 15.7 %copy-start = (bf16[3584,8]{0,1:T(8,128)(2,1)S(1)}, bf16[3584,8]{0,1:T(8,128)(2,1)}, u32[]{:S(2)}) copy-start(bf16[3584,8]{0,1:T(8,128)(2,1)} %param.15) | copy-start | bytes 172036
  13.5 1.2 copy-start.2
  14.7 0.7 copy-start.4
  14.7 0.7 copy-start.3
  15.7 1.0 copy-start.1

commit v4 on v3

--- a/solution.py
+++ b/solution.py
@@ -483,14 +483,23 @@
     low_half = z < length // 2
 
     def one_round(away, carry):
-        @pl.when(away < length)
-        def _():
-            def both_pieces(piece, inner):
+        def both_pieces(piece, inner):
+            far = away - 2
+
+            @pl.when(far > 0)
+            def _():
+                return_up(far, piece, low_half)
+                return_down(length - 1 - far, piece, True)
+                return_up(far, piece, jnp.logical_not(low_half))
+
+            @pl.when(away < length)
+            def _():
                 gather_piece(z - away, piece)
                 gather_piece(z + away, piece)
-                return inner
-
-            lax.fori_loop(0, PIECES, both_pieces, 0)
+
+            return inner
+
+        lax.fori_loop(0, PIECES, both_pieces, 0)
 
         def near_block(which, inner):
             at = jnp.where(which == 0, z - away + 1, z + away - 1)
@@ -502,17 +511,6 @@
             return inner
 
         lax.fori_loop(0, 2, near_block, 0)
-
-        def return_piece(piece, inner):
-            far = away - 2
-            return_up(far, piece, low_half)
-            return_down(length - 1 - far, piece, True)
-            return_up(far, piece, jnp.logical_not(low_half))
-            return inner
-
-        @pl.when(away > 2)
-        def _():
-            lax.fori_loop(0, PIECES, return_piece, 0)
 
         return carry
 

time: 225 us -> 199 us (0.88)
  Pallas kernels: 213 us -> 187 us
    pallas_call x1, Pallas kernels: 205 us -> 179 us  [routed_experts(): pl.pallas_call(functools.partial(expert_kernel, owners), in_specs=[anywhe...]
where the time goes in v4:
time: 199 us; the launch traced here: 198 us
  Pallas kernels  187 us (94%)
  blocking collectives  5.57 us (3%)
  other arithmetic  3.76 us (2%)
    pallas_call x1, Pallas kernels, routed_experts(): pl.pallas_call(functools.partial(expert_kernel, owners), in_specs=[anywhe...  179 us
    pallas_call x1, Pallas kernels, attention(): pl.pallas_call(attention_kernel, grid=(cols // width,), in_specs=[spec] *...  7.78 us
    all_to_all x1, blocking collectives, hidden_and_normed(): lax.all_to_all(attention(queries, key_rows, value_rows), 'seq', split_axi...  5.57 us

profile of v4, /device:TPU:0, one launch (start us, length us, event | category | flops | bytes accessed | tf_op | source)
XLA Modules:
  0.0 198.1 jit_solution(17730206217871879841)
XLA Ops:
  0.0 0.0 copy-start
  0.0 7.8 %shard_map.100 = bf16[256,1792]{1,0:T(8,128)(2,1)} custom-call(bf16[256,1792]{1,0:T(8,128)(2,1)} %q_ref.1, bf16[256,1792]{1,0:T(8,128)(2,1)} %k_ref.1, bf16[256,1792]{1,0:T(8,128)(2,1)} %v_ref.1), custom_call_target="tpu_custom_call" | custom-call | flops 469762048 | bytes 3670016 | tf_op jit(solution)/shard_map/pallas_call | solution.py:137
  7.8 5.6 %all_to_all.13 = bf16[2,128,1792]{2,1,0:T(8,128)(2,1)S(1)} all-to-all(bf16[2,128,1792]{2,1,0:T(8,128)(2,1)} %bitcast.13), channel_id=1, replica_groups=mesh['groups'=2,'exp'=8,'seq'=2] {'seq'}, dimensions={0} | all-to-all | bytes 1835008 | tf_op jit(solution)/shard_map/all_to_all | solution.py:152
  13.3 0.1 convert_bitcast_fusion
  13.5 0.0 copy-start.2
  13.5 0.2 copy.16
  13.7 1.0 copy-done.2
  14.7 0.0 copy-start.4
  14.7 0.0 copy-start.3
  14.7 0.4 fusion
  15.0 0.3 copy-done.4
  15.3 0.0 copy-done.3
  15.4 0.3 fusion.2.normed_ref
  15.7 0.0 copy-done
  15.7 0.0 copy-start.1
  15.7 0.4 fusion.9
  16.1 0.6 divide_bitcast_fusion.gates_ref
  16.7 0.0 copy-done.1
  16.7 179.0 %shard_map.101 = bf16[128,3584]{1,0:T(8,128)(2,1)} custom-call(bf16[128,3584]{1,0:T(8,128)(2,1)} %copy-done.1, f32[8,128]{1,0:T(8,128)} %divide_bitcast_fusion.gates_ref, bf16[3584,384]{1,0:T(8,128)(2,1)} %bitcast.14, bf16[3584,384]{1,0:T(8,128)(2,1)} %bitcast.15, bf16[384,3584]{1,0:T(8,128)(2,1)} %bitcast.16), custom_call_target="tpu_custom_call" | custom-call | flops 16911433728 | bytes 16515072 | tf_op jit(solution)/shard_map/pallas_call | solution.py:589
  195.7 2.4 %fusion.3 = bf16[128,3584]{1,0:T(8,128)(2,1)} fusion(bf16[128,3584]{1,0:T(8,128)(2,1)S(1)} %get-tuple-element.6, bf16[128,3584]{1,0:T(8,128)(2,1)} %shard_map.101), kind=kLoop, calls=%fused_computation.6 | loop fusion | flops 1835008 | bytes 2752512 | tf_op jit(solution)/shard_map/convert_element_type | solution.py:641
  (2 shorter events, 0.0 us)
Async XLA Ops:
  0.0 15.7 %copy-start = (bf16[3584,8]{0,1:T(8,128)(2,1)S(1)}, bf16[3584,8]{0,1:T(8,128)(2,1)}, u32[]{:S(2)}) copy-start(bf16[3584,8]{0,1:T(8,128)(2,1)} %param.15) | copy-start | bytes 172036
  13.5 1.2 copy-start.2
  14.7 0.7 copy-start.4
  14.7 0.7 copy-start.3
  15.7 1.0 copy-start.1
